TPU v7x, 512 devices: a whole 4x8x8 slice. The times are simulated.
512 devices in a mesh: slab: 16 (over y_lo, z), group: 32 (over x, y_hi, core).
Axes of the slice: x: 4, y: 8 (y_hi: 4, y_lo: 2; y = y_hi * 2 + y_lo), z: 8, core: 2. Of those that a mesh axis runs over, the one named last changes fastest.
Arguments:
- images: bfloat16 [131072, 768], P(('slab', 'group')), may hold values from -200 to 200
- references: bfloat16 [8192, 768], P(('slab', 'group')), may hold values from -4 to 4
- ctf_table: float32 [32, 384], replicated, may hold values from -1.3 to 1.3
- ctf_ids: int32 [131072], P(('slab', 'group')), may hold values from 0 to 31
- owners: int32 [131072], P(('slab', 'group')), may hold values from 0 to 15, as said below
Outputs:
- new_references: float32 [8192, 768], P(('slab', 'group'))
- log_evidence: float32 [131072], P(('slab', 'group'))
Inputs may be any that keep to these rules, and one draw needn't show every extreme that they name: `owners`: no slab is named by more than 48 lines of one device's 256, and in every device's lines one slab is named by exactly 48.
All inputs are finite; a program needn't handle non-finite values.
Results may differ from a plain program's by a relative error of at most 0.003.
Values may be sent and summed in bfloat16 or wider, within the bound.
A program may use at most 64 MiB of HBM per device.

v0:
```python
import jax
import jax.numpy as jnp
from jax import lax
from jax.sharding import PartitionSpec as P


def slot_plan(owner_block, slab_count, capacity):
    line_count = owner_block.shape[0]
    one_hot = (owner_block[:, None] == jnp.arange(slab_count, dtype=jnp.int32)[None, :]).astype(
        jnp.int32
    )
    earlier = jnp.cumsum(one_hot, axis=0) - one_hot
    rank_index = jnp.sum(earlier * one_hot, axis=1)
    slot_index = owner_block * capacity + rank_index
    filled_slot = (
        jnp.zeros((slab_count * capacity,), jnp.int32)
        .at[slot_index]
        .set(jnp.arange(line_count, dtype=jnp.int32) + 1)
    )
    filled_mask = filled_slot > 0
    source_row = jnp.maximum(filled_slot - 1, 0)
    return (slot_index, source_row, filled_mask)


def weigh(image_slots, ctf_tags, ctf_table):
    group_count = ctf_table.shape[0]
    levels = jnp.arange(1, group_count + 1, dtype=jnp.float32)
    group_pick = (ctf_tags.astype(jnp.float32)[:, None] == levels[None, :]).astype(jnp.float32)
    ctf_rows = jnp.dot(group_pick, ctf_table, precision=lax.Precision.HIGHEST)
    weighted = (
        image_slots.astype(jnp.float32) * jnp.concatenate([ctf_rows, ctf_rows], axis=1)
    ).astype(jnp.bfloat16)
    ctf_square = (ctf_rows * ctf_rows).astype(jnp.bfloat16)
    return (weighted, ctf_square)


def score_block(weighted, ctf_square, ref_lines):
    half_width = ref_lines.shape[1] // 2
    widened = ref_lines.astype(jnp.float32)
    line_power = (widened[:, :half_width] ** 2 + widened[:, half_width:] ** 2).astype(jnp.bfloat16)
    cross_term = lax.dot_general(
        weighted, ref_lines, (((1,), (1,)), ((), ())), preferred_element_type=jnp.float32
    )
    quad_term = lax.dot_general(
        ctf_square, line_power, (((1,), (1,)), ((), ())), preferred_element_type=jnp.float32
    )
    return (cross_term - 0.5 * quad_term) * ref_lines.shape[1] ** (-0.5)


def on_device(images, references, ctf_table, ctf_ids, owners):
    slab_count = lax.axis_size("slab")
    line_count = images.shape[0]
    capacity = 3 * line_count // slab_count
    slot_index, source_row, filled_mask = slot_plan(owners, slab_count, capacity)
    image_slots = jnp.where(filled_mask[:, None], images[source_row], jnp.zeros((), jnp.bfloat16))
    ctf_tags = jnp.where(filled_mask, ctf_ids[source_row] + 1, 0).astype(jnp.bfloat16)
    arrived_lines, arrived_tags = (
        lax.all_to_all(image_slots, "slab", split_axis=0, concat_axis=0, tiled=True),
        lax.all_to_all(ctf_tags, "slab", split_axis=0, concat_axis=0, tiled=True),
    )
    weighted, ctf_square = weigh(arrived_lines, arrived_tags, ctf_table)
    arrived_mask = arrived_tags.astype(jnp.float32) > 0.0
    scores = score_block(
        weighted, ctf_square, lax.all_gather(references, "group", axis=0, tiled=True)
    )
    score_max = jnp.max(scores, axis=1, keepdims=True)
    exp_total = jnp.sum(jnp.exp(scores - score_max), axis=1, keepdims=True)
    evidence = score_max + jnp.log(exp_total)
    responsibility = (
        jnp.exp(scores - evidence) * arrived_mask[:, None].astype(jnp.float32)
    ).astype(jnp.bfloat16)
    numerator = lax.dot_general(
        responsibility, weighted, (((0,), (0,)), ((), ())), preferred_element_type=jnp.float32
    )
    denominator = lax.dot_general(
        responsibility, ctf_square, (((0,), (0,)), ((), ())), preferred_element_type=jnp.float32
    )
    returned = lax.all_to_all(evidence[:, 0], "slab", split_axis=0, concat_axis=0, tiled=True)
    line_evidence = returned[slot_index]
    summed_num, summed_den = lax.psum((numerator, denominator), "group")
    share_rows = numerator.shape[0] // lax.axis_size("group")
    offset = lax.axis_index("group") * share_rows
    share_num = lax.dynamic_slice_in_dim(summed_num, offset, share_rows, 0)
    share_den = lax.dynamic_slice_in_dim(summed_den, offset, share_rows, 0)
    new_references = share_num / (jnp.concatenate([share_den, share_den], axis=1) + 1.0)
    return (new_references, line_evidence)


def solution(mesh):
    in_specs = (
        P(("slab", "group"), None),
        P(("slab", "group"), None),
        P(),
        P(("slab", "group")),
        P(("slab", "group")),
    )
    out_specs = (P(("slab", "group"), None), P(("slab", "group")))
    return jax.shard_map(
        on_device, mesh=mesh, in_specs=in_specs, out_specs=out_specs, check_vma=False
    )
```

profile of v0, /device:TPU:1, one launch (start us, length us, event | category | flops | bytes accessed | tf_op | source)
XLA Modules:
  0.0 413.9 jit_solution(3139050886746585395)
XLA Ops:
  7.2 0.7 fusion.14
  7.9 0.6 reduce-window.6
  8.7 0.8 fusion.13
  9.5 0.7 compare_select_fusion
  10.2 1.4 scatter_custom_fusion
  11.6 5.0 %gather_fusion.1 = s32[768]{0:T(1024)S(1)} fusion(s32[256]{0:T(256)S(1)} %copy-done.1, s32[1024]{0:T(1024)S(1)} %pad_clamp_fusion.1), kind=kCustom, calls=%fused_computation.1 | custom fusion | bytes 9216 | tf_op jit(solution)/shard_map/gather | solution.py:56
  16.6 0.7 all_to_all.21
  17.3 12.0 %all-to-all-start.1 = ((bf16[16,48,1]{1,2,0:T(2,128)(2,1)}), bf16[16,48,1]{1,2,0:T(2,128)(2,1)S(1)}, u32[]{:S(2)}, u32[]{:S(2)}) async-start(bf16[16,48,1]{1,2,0:T(2,128)(2,1)} %all_to_all.21), calls=%async_computation.1 | async-start | bytes 16384 | tf_op jit(solution)/shard_map/all_to_all | solution.py:59
  29.4 2.8 gather_fusion
  32.2 1.2 broadcast_select_fusion
  33.4 3.2 all-to-all-done.1
  36.5 4.5 %all-to-all-start = ((bf16[16,48,768]{2,1,0:T(8,128)(2,1)}), bf16[16,48,768]{2,1,0:T(8,128)(2,1)S(1)}, u32[]{:S(2)}, u32[]{:S(2)}) async-start(bf16[16,48,768]{2,1,0:T(8,128)(2,1)} %broadcast_select_fusion), calls=%async_computation | async-start | bytes 2359296 | tf_op jit(solution)/shard_map/all_to_all | solution.py:58
  41.1 56.4 %all_gather.3 = bf16[512,768]{1,0:T(8,128)(2,1)S(1)} all-gather(bf16[16,768]{1,0:T(8,128)(2,1)S(1)} %copy-done.4), channel_id=1, replica_groups=mesh['slab'=16,'group'=32] {'group'}, dimensions={0}, use_global_device_ids=true | all-gather | bytes 811008 | tf_op jit(solution)/shard_map/all_gather | solution.py:64
  97.5 1.3 convert_element_type.63
  98.8 0.5 iota_add_fusion.1
  99.4 1.6 fusion.4
  101.1 1.6 bitcast_convert_fusion
  102.7 3.1 copy.12
  105.8 2.7 fusion.18
  108.5 0.6 fusion.20
  109.4 0.8 copy-done.2
  110.1 2.1 fusion.9
  112.2 1.5 fusion.6
  113.8 0.7 add.77
  114.4 7.5 %all-to-all-start.2 = ((f32[16,48,1]{1,2,0:T(1,128)}), f32[16,48,1]{1,2,0:T(1,128)S(1)}, u32[]{:S(2)}, u32[]{:S(2)}) async-start(f32[16,48,1]{1,2,0:T(1,128)} %bitcast.4), calls=%async_computation.2 | async-start | bytes 16384 | tf_op jit(solution)/shard_map/all_to_all | solution.py:78
  122.0 7.3 %all-to-all-done.2 = f32[16,48,1]{1,2,0:T(1,128)S(1)} async-done(((f32[16,48,1]{1,2,0:T(1,128)}), f32[16,48,1]{1,2,0:T(1,128)S(1)}, u32[]{:S(2)}, u32[]{:S(2)}) %all-to-all-start.2) | async-done | bytes 3104 | tf_op jit(solution)/shard_map/all_to_all | solution.py:78
  129.3 0.5 broadcast.79
  129.8 0.7 reduce.9
  130.6 1.9 gather_fusion.2
  132.5 272.4 %all-reduce.3.cloned.1.call-done = (f32[512,384]{1,0:T(8,128)}, f32[512,768]{1,0:T(8,128)}) async-done(((f32[512,384]{1,0:T(8,128)}, f32[512,768]{1,0:T(8,128)}), (f32[512,384]{1,0:T(8,128)}, f32[512,768]{1,0:T(8,128)})) %all-reduce.3.cloned.1.call-update) | async-done | bytes 2359312 | tf_op jit(solution)/shard_map/psum | solution.py:80
  404.9 0.7 constant_dynamic-slice_fusion
  405.6 1.4 fusion.10
  (26 shorter events, 0.9 us)
Async XLA Ops:
  7.2 22.2 %copy-start = (bf16[256,768]{1,0:T(8,128)(2,1)S(1)}, bf16[256,768]{1,0:T(8,128)(2,1)}, u32[]{:S(2)}) copy-start(bf16[256,768]{1,0:T(8,128)(2,1)} %param.5) | copy-start | bytes 1179652
  7.2 4.4 %copy-start.1 = (s32[256]{0:T(256)S(1)}, s32[256]{0:T(256)}, u32[]{:S(2)}) copy-start(s32[256]{0:T(256)} %param.8) | copy-start | bytes 3076
  17.3 19.2 %all-to-all-start.1 = ((bf16[16,48,1]{1,2,0:T(2,128)(2,1)}), bf16[16,48,1]{1,2,0:T(2,128)(2,1)S(1)}, u32[]{:S(2)}, u32[]{:S(2)}) async-start(bf16[16,48,1]{1,2,0:T(2,128)(2,1)} %all_to_all.21), calls=%async_computation.1 | async-start | bytes 16384 | tf_op jit(solution)/shard_map/all_to_all | solution.py:59
  33.4 7.8 %copy-start.4 = (bf16[16,768]{1,0:T(8,128)(2,1)S(1)}, bf16[16,768]{1,0:T(8,128)(2,1)}, u32[]{:S(2)}) copy-start(bf16[16,768]{1,0:T(8,128)(2,1)} %param.6) | copy-start | bytes 73732
  36.5 64.5 %all-to-all-start = ((bf16[16,48,768]{2,1,0:T(8,128)(2,1)}), bf16[16,48,768]{2,1,0:T(8,128)(2,1)S(1)}, u32[]{:S(2)}, u32[]{:S(2)}) async-start(bf16[16,48,768]{2,1,0:T(8,128)(2,1)} %broadcast_select_fusion), calls=%async_computation | async-start | bytes 2359296 | tf_op jit(solution)/shard_map/all_to_all | solution.py:58
  41.1 363.8 %all-reduce.3.cloned.1.call-start = ((), (), s32[]{:S(2)}) async-start(), calls=%async_computation.3 | async-start | bytes 4718592 | tf_op jit(solution)/shard_map/psum | solution.py:80
  105.8 2.7 copy-start.3
  108.5 1.7 copy-start.2
  114.4 14.9 %all-to-all-start.2 = ((f32[16,48,1]{1,2,0:T(1,128)}), f32[16,48,1]{1,2,0:T(1,128)S(1)}, u32[]{:S(2)}, u32[]{:S(2)}) async-start(f32[16,48,1]{1,2,0:T(1,128)} %bitcast.4), calls=%async_computation.2 | async-start | bytes 16384 | tf_op jit(solution)/shard_map/all_to_all | solution.py:78
Sparse Core Ops, SparseCore 0:
  113.9 290.9 all-reduce.2
where the time goes:
time: 415 us; the launch traced here: 414 us
  waiting for transfers between devices  283 us (68%)
  blocking collectives  56.4 us (14%)
  starting transfers between devices  24 us (6%)
  local copies, waits for them, and re-layouts  18 us (4%)
  between operations  14.2 us (3%)
  other arithmetic  9.84 us (2%)
  matrix products  8.53 us (2%)
    psum x1, waiting for transfers between devices, on_device(): summed_num, summed_den = lax.psum((numerator, denominator), 'group')  272 us
    all_gather x1, blocking collectives, on_device(): lax.all_gather(references, 'group', axis=0, tiled=True)  56.4 us
    all_to_all x1, starting transfers between devices, on_device(): lax.all_to_all(ctf_tags, 'slab', split_axis=0, concat_axis=0, tiled=True)  12 us
  transfers between devices with their start and end apart: 4, of which 3 were waited for; matrix products, arithmetic and copies ran while one was open for 3% of the time, Pallas kernels for 0%

commit v1 on v0

--- a/solution.py
+++ b/solution.py
@@ -2,6 +2,16 @@
 import jax.numpy as jnp
 from jax import lax
 from jax.sharding import PartitionSpec as P
+
+carry_scenes = lambda net_axis, target: jnp.concatenate(
+    lax.all_to_all(
+        jnp.stack([target for _ in range(lax.axis_size(net_axis))]),
+        net_axis,
+        concat_axis=0,
+        split_axis=0,
+    ),
+    axis=0,
+)
 
 
 def slot_plan(owner_block, slab_count, capacity):
@@ -60,9 +70,7 @@
     )
     weighted, ctf_square = weigh(arrived_lines, arrived_tags, ctf_table)
     arrived_mask = arrived_tags.astype(jnp.float32) > 0.0
-    scores = score_block(
-        weighted, ctf_square, lax.all_gather(references, "group", axis=0, tiled=True)
-    )
+    scores = score_block(weighted, ctf_square, carry_scenes("group", references))
     score_max = jnp.max(scores, axis=1, keepdims=True)
     exp_total = jnp.sum(jnp.exp(scores - score_max), axis=1, keepdims=True)
     evidence = score_max + jnp.log(exp_total)

time: 415 us -> 412 us (level)
  waiting for transfers between devices: 283 us -> 327 us
  blocking collectives: 56.4 us -> 19.1 us
    all_gather x1 -> x0, blocking collectives: 56.4 us -> none  [on_device(): lax.all_gather(references, 'group', axis=0, tiled=True)]
    all_to_all x1, waiting for transfers between devices: 0.01 us -> 25.2 us  [on_device(): lax.all_to_all(image_slots, 'slab', split_axis=0, concat_axis=0, tiled=True)]
    all_to_all x0 -> x1, blocking collectives: none -> 19.1 us  [on_device(): lax.all_to_all(ctf_tags, 'slab', split_axis=0, concat_axis=0, tiled=True)]
    all_to_all x1, waiting for transfers between devices: 3.18 us -> 19 us  [lax.all_to_all(jnp.stack([target for _ in range(lax.axis_size(net_axis))]...]
  transfers between devices with their start and end apart: 4 -> 4, of which waited for: 3 -> 4; matrix products, arithmetic and copies ran while one was open for 3% -> 3% of each run, Pallas kernels for 0% -> 0%
where the time goes in v1:
time: 412 us
  waiting for transfers between devices  327 us (79%)
  starting transfers between devices  21.5 us (5%)
  blocking collectives  19.1 us (5%)
  local copies, waits for them, and re-layouts  15 us (4%)
  between operations  14.2 us (3%)
  other arithmetic  8.18 us (2%)
  matrix products  6.36 us (2%)
    psum x1, waiting for transfers between devices, on_device(): summed_num, summed_den = lax.psum((numerator, denominator), 'group')  276 us
    all_to_all x1, waiting for transfers between devices, on_device(): lax.all_to_all(image_slots, 'slab', split_axis=0, concat_axis=0, tiled=True)  25.2 us
    all_to_all x1, blocking collectives, on_device(): lax.all_to_all(ctf_tags, 'slab', split_axis=0, concat_axis=0, tiled=True)  19.1 us
    all_to_all x1, waiting for transfers between devices, lax.all_to_all(jnp.stack([target for _ in range(lax.axis_size(net_axis))]...  19 us
    all_to_all x1, starting transfers between devices, lax.all_to_all(jnp.stack([target for _ in range(lax.axis_size(net_axis))]...  10.9 us
  transfers between devices with their start and end apart: 4, of which 4 were waited for; matrix products, arithmetic and copies ran while one was open for 3% of the time, Pallas kernels for 0%

profile of v1, /device:TPU:1, one launch (start us, length us, event | category | flops | bytes accessed | tf_op | source)
XLA Modules:
  0.0 411.8 jit_solution(14866728140728733923)
XLA Ops:
  7.2 0.7 fusion.15
  7.9 0.6 reduce-window.6
  8.7 0.8 fusion.14
  9.5 0.7 compare_select_fusion
  10.2 1.4 scatter_custom_fusion
  11.6 5.0 %gather_fusion.1 = s32[768]{0:T(1024)S(1)} fusion(s32[256]{0:T(256)S(1)} %copy-done.1, s32[1024]{0:T(1024)S(1)} %pad_clamp_fusion.1), kind=kCustom, calls=%fused_computation.1 | custom fusion | bytes 9216 | tf_op jit(solution)/shard_map/gather | solution.py:66
  16.7 19.1 %all_to_all.30 = bf16[16,48,1]{1,2,0:T(2,128)(2,1)S(1)} all-to-all(bf16[16,48,1]{1,2,0:T(2,128)(2,1)S(1)} %all_to_all.25), channel_id=1, replica_groups=mesh['slab'=16,'group'=32] {'slab'}, dimensions={0} | all-to-all | bytes 3072 | tf_op jit(solution)/shard_map/all_to_all | solution.py:69
  35.8 0.9 stack.2
  36.7 10.9 %all-to-all-start.2 = ((bf16[32,16,768]{2,1,0:T(8,128)(2,1)}), bf16[32,16,768]{2,1,0:T(8,128)(2,1)S(1)}, u32[]{:S(2)}, u32[]{:S(2)}) async-start(bf16[32,16,768]{2,1,0:T(8,128)(2,1)} %stack.2), calls=%async_computation.2 | async-start | bytes 1572864 | tf_op jit(solution)/shard_map/all_to_all | solution.py:7
  47.8 2.8 gather_fusion
  50.5 1.2 broadcast_select_fusion
  51.7 19.0 %all-to-all-done.2 = bf16[32,16,768]{2,1,0:T(8,128)(2,1)S(1)} async-done(((bf16[32,16,768]{2,1,0:T(8,128)(2,1)}), bf16[32,16,768]{2,1,0:T(8,128)(2,1)S(1)}, u32[]{:S(2)}, u32[]{:S(2)}) %all-to-all-start.2) | async-done | bytes 786464 | tf_op jit(solution)/shard_map/all_to_all | solution.py:7
  70.8 3.7 all-to-all-start
  74.7 1.5 fusion.5
  76.1 1.3 bitcast_convert_fusion
  77.4 25.2 %all-to-all-done = bf16[16,48,768]{2,1,0:T(8,128)(2,1)S(1)} async-done(((bf16[16,48,768]{2,1,0:T(8,128)(2,1)}), bf16[16,48,768]{2,1,0:T(8,128)(2,1)S(1)}, u32[]{:S(2)}, u32[]{:S(2)}) %all-to-all-start) | async-done | bytes 1179680 | tf_op jit(solution)/shard_map/all_to_all | solution.py:68
  102.7 0.2 fusion
  102.9 0.8 fusion.19
  103.7 0.6 copy-done.2
  104.3 0.6 fusion.18
  104.9 0.3 exponential_reduce_fusion
  105.2 1.5 fusion.7
  106.9 2.0 fusion.10
  108.9 0.7 add.77
  109.6 6.8 %all-to-all-start.3 = ((f32[16,48,1]{1,2,0:T(1,128)}), f32[16,48,1]{1,2,0:T(1,128)S(1)}, u32[]{:S(2)}, u32[]{:S(2)}) async-start(f32[16,48,1]{1,2,0:T(1,128)} %bitcast.7), calls=%async_computation.3 | async-start | bytes 16384 | tf_op jit(solution)/shard_map/all_to_all | solution.py:86
  116.4 7.2 %all-to-all-done.3 = f32[16,48,1]{1,2,0:T(1,128)S(1)} async-done(((f32[16,48,1]{1,2,0:T(1,128)}), f32[16,48,1]{1,2,0:T(1,128)S(1)}, u32[]{:S(2)}, u32[]{:S(2)}) %all-to-all-start.3) | async-done | bytes 3104 | tf_op jit(solution)/shard_map/all_to_all | solution.py:86
  123.6 0.5 broadcast.81
  124.1 0.7 reduce.9
  124.9 1.9 gather_fusion.2
  126.8 276.0 %all-reduce.3.cloned.1.call-done = (f32[512,384]{1,0:T(8,128)}, f32[512,768]{1,0:T(8,128)}) async-done(((f32[512,384]{1,0:T(8,128)}, f32[512,768]{1,0:T(8,128)}), (f32[512,384]{1,0:T(8,128)}, f32[512,768]{1,0:T(8,128)})) %all-reduce.3.cloned.1.call-update) | async-done | bytes 2359312 | tf_op jit(solution)/shard_map/psum | solution.py:88
  402.8 0.7 constant_dynamic-slice_fusion
  403.5 1.4 fusion.11
  (25 shorter events, 0.9 us)
Async XLA Ops:
  7.2 40.6 %copy-start = (bf16[256,768]{1,0:T(8,128)(2,1)S(1)}, bf16[256,768]{1,0:T(8,128)(2,1)}, u32[]{:S(2)}) copy-start(bf16[256,768]{1,0:T(8,128)(2,1)} %param.5) | copy-start | bytes 1179652
  7.2 4.4 %copy-start.1 = (s32[256]{0:T(256)S(1)}, s32[256]{0:T(256)}, u32[]{:S(2)}) copy-start(s32[256]{0:T(256)} %param.8) | copy-start | bytes 3076
  11.6 24.2 %copy-start.3 = (bf16[16,768]{1,0:T(8,128)(2,1)S(1)}, bf16[16,768]{1,0:T(8,128)(2,1)}, u32[]{:S(2)}) copy-start(bf16[16,768]{1,0:T(8,128)(2,1)} %param.6) | copy-start | bytes 73732
  36.7 34.0 %all-to-all-start.2 = ((bf16[32,16,768]{2,1,0:T(8,128)(2,1)}), bf16[32,16,768]{2,1,0:T(8,128)(2,1)S(1)}, u32[]{:S(2)}, u32[]{:S(2)}) async-start(bf16[32,16,768]{2,1,0:T(8,128)(2,1)} %stack.2), calls=%async_computation.2 | async-start | bytes 1572864 | tf_op jit(solution)/shard_map/all_to_all | solution.py:7
  70.8 31.9 %all-to-all-start = ((bf16[16,48,768]{2,1,0:T(8,128)(2,1)}), bf16[16,48,768]{2,1,0:T(8,128)(2,1)S(1)}, u32[]{:S(2)}, u32[]{:S(2)}) async-start(bf16[16,48,768]{2,1,0:T(8,128)(2,1)} %broadcast_select_fusion), calls=%async_computation | async-start | bytes 2359296 | tf_op jit(solution)/shard_map/all_to_all | solution.py:68
  74.5 328.3 %all-reduce.3.cloned.1.call-start = ((), (), s32[]{:S(2)}) async-start(), calls=%async_computation.4 | async-start | bytes 4718592 | tf_op jit(solution)/shard_map/psum | solution.py:88
  102.9 1.4 copy-start.2
  109.6 14.0 %all-to-all-start.3 = ((f32[16,48,1]{1,2,0:T(1,128)}), f32[16,48,1]{1,2,0:T(1,128)S(1)}, u32[]{:S(2)}, u32[]{:S(2)}) async-start(f32[16,48,1]{1,2,0:T(1,128)} %bitcast.7), calls=%async_computation.3 | async-start | bytes 16384 | tf_op jit(solution)/shard_map/all_to_all | solution.py:86
Sparse Core Ops, SparseCore 0:
  109.0 293.7 all-reduce.2
